TPU v7x, 32 devices: a whole 2x2x4 slice. The times are simulated.
32 devices in a mesh: wave: 8 (over z, y), lev: 4 (over x, core).
Axes of the slice: x: 2, y: 2, z: 4, core: 2. Of those that a mesh axis runs over, the one named last changes fastest.
Arguments:
- spectral: bfloat16 [1280, 256, 1280], P('wave', 'lev'), may hold values from -6 to 6
- legendre: bfloat16 [1280, 32, 1280], P('wave'), may hold values from -0.0034179688 to 0.0034179688
- wave_map: int32 [1280], replicated, may hold values from 0 to 1279, each once
- row_points: int32 [32], replicated, may hold values from 20 to 5136, as said below
- brackets: int32 [4], replicated, may hold values from 0 to 14, as said below
- lev_weight: float32 [4], replicated, may hold values from 0.05 to 0.95
- climatology: float32 [4, 64, 5248], P('lev', 'wave'), may hold values from 0.1 to 1
Outputs:
- anomaly: float32 [4, 64, 5248], P('lev', 'wave')
Inputs may be any that keep to these rules, and one draw needn't show every extreme that they name: `wave_map`: each wavenumber once. `row_points`: each is 20 + 4 i for a whole number i below 1280; some row has 5136 points. `brackets`: pressure level p has its lower bracket level among the 4 model levels of band p (levels b * 4 to b * 4 + 3 for band b); some pressure level outside the last band takes the last level of its band; the last pressure level takes 16 - 2.
All inputs are finite; a program needn't handle non-finite values.
Results may differ from a plain program's by a relative error of at most 0.0003.
Values sent between devices are 32-bit elements; how exact they have to be, the bound alone decides.
No kernel may reach another device: no remote copies, remote signals or barrier semaphores. Data moves between devices by JAX's collectives and lax.ppermute only.
A program may use at most 256 MiB of HBM per device.

v0:
```python
import math

import jax
import jax.numpy as jnp
from jax import lax
from jax.sharding import PartitionSpec as P

M = 1280
NT = 1280
LEV_DEV = 4
STEPS = 4
FIELDS = 2
ROWPAD = 5248


TWO_PI = 2.0 * math.pi


def synthesize(coeffs, wave_map, points):
    places = jnp.arange(ROWPAD, dtype=jnp.int32)
    fine_ids = jnp.arange(64, dtype=jnp.int32)
    coarse_ids = jnp.arange(M // 64, dtype=jnp.int32) * 64
    step_rad = TWO_PI / points.astype(jnp.float32)
    fine_angle = (fine_ids[:, None] * places[None, :] % points).astype(jnp.float32) * step_rad
    coarse_angle = (coarse_ids[:, None] * places[None, :] % points).astype(jnp.float32) * step_rad
    fine_cos = jnp.cos(fine_angle)[None, :, :]
    fine_sin = jnp.sin(fine_angle)[None, :, :]
    coarse_cos = jnp.cos(coarse_angle)[:, None, :]
    coarse_sin = jnp.sin(coarse_angle)[:, None, :]
    cosine = (coarse_cos * fine_cos - coarse_sin * fine_sin).reshape(M, ROWPAD)
    sine_part = (coarse_sin * fine_cos + coarse_cos * fine_sin).reshape(M, ROWPAD)
    orders = jnp.arange(M, dtype=jnp.int32)
    factor = jnp.where(orders == 0, 1.0, 2.0).astype(jnp.float32)
    factor = jnp.where(orders <= (points - 1) // 2, factor, 0.0)
    ordered = jnp.zeros_like(coeffs).at[wave_map].set(coeffs) * factor[:, None, None]
    real_part = lax.dot_general(
        ordered[:, :, 0],
        cosine,
        (((0,), (0,)), ((), ())),
        precision=lax.Precision.HIGHEST,
        preferred_element_type=jnp.float32,
    )
    imag_part = lax.dot_general(
        ordered[:, :, 1],
        sine_part,
        (((0,), (0,)), ((), ())),
        precision=lax.Precision.HIGHEST,
        preferred_element_type=jnp.float32,
    )
    return jnp.where(places[None, :] < points, real_part - imag_part, 0.0)


def kinetic(values):
    return 0.5 * jnp.mean(values[:, 0] * values[:, 0] + values[:, 1] * values[:, 1], axis=1)


def mixing_table(brackets, lev_weight, levels_all):
    level_ids = jnp.arange(levels_all, dtype=jnp.int32)
    lower_hit = (level_ids[None, :] == brackets[:, None]).astype(jnp.float32)
    upper_hit = (level_ids[None, :] == brackets[:, None] + 1).astype(jnp.float32)
    return lev_weight[:, None] * lower_hit + (1.0 - lev_weight[:, None]) * upper_hit


def local(spectral, legendre, wave_map, row_points, brackets, lev_weight, climatology):
    slot_count = spectral.shape[0]
    half_rows = legendre.shape[1]
    lat_total = 2 * half_rows
    wave_idx = lax.axis_index("wave")
    lev_idx = lax.axis_index("lev")
    wave_count = lax.axis_size("wave")
    lev_count = lax.axis_size("lev")
    band_rows = lat_total // wave_count
    levels_all = LEV_DEV * lev_count
    plev_all = brackets.shape[0]
    width_q = FIELDS * STEPS * 2
    mixing = mixing_table(brackets, lev_weight, levels_all)
    points_all = jnp.concatenate([row_points, row_points])
    own_waves = lax.dynamic_slice_in_dim(wave_map, wave_idx * slot_count, slot_count, 0)
    degree = jnp.arange(NT, dtype=jnp.int32)
    kept_mask = degree[None, :] >= own_waves[:, None]
    parity = (1 - 2 * ((degree[None, :] + own_waves[:, None]) % 2)).astype(jnp.bfloat16)
    plain_coeffs = jnp.where(kept_mask[:, None, :], spectral, jnp.zeros((), jnp.bfloat16))
    signed = plain_coeffs * parity[:, None, :]
    north_part = jnp.einsum(
        "scn,sjn->scj", plain_coeffs, legendre, preferred_element_type=jnp.float32
    )
    south_part = jnp.einsum("scn,sjn->scj", signed, legendre, preferred_element_type=jnp.float32)
    fourier = jnp.concatenate([north_part, south_part], axis=2)
    moved_coeffs = lax.all_to_all(
        lax.all_to_all(fourier, "wave", split_axis=2, concat_axis=0, tiled=True),
        "lev",
        split_axis=2,
        concat_axis=1,
        tiled=True,
    )
    rows_here = moved_coeffs.shape[2]
    first_row = wave_idx * band_rows + lev_idx * rows_here

    def grid_row(row_input):
        row_coeffs, points = row_input
        split_cols = row_coeffs.reshape(M, levels_all, width_q)
        mixed_cols = jnp.einsum("pl,mlq->mpq", mixing, split_cols, precision=lax.Precision.HIGHEST)
        values = synthesize(mixed_cols.reshape(M, plev_all * FIELDS * STEPS, 2), wave_map, points)
        values = values.reshape(plev_all, FIELDS, STEPS, ROWPAD)
        return kinetic(values)

    row_points_here = lax.dynamic_slice_in_dim(points_all, first_row, rows_here, 0)
    energy_rows = lax.map(grid_row, (jnp.moveaxis(moved_coeffs, 2, 0), row_points_here))
    energy_rows = jnp.transpose(energy_rows, (1, 0, 2))
    result = lax.all_to_all(energy_rows, "lev", split_axis=0, concat_axis=1, tiled=True)
    out_points = lax.dynamic_slice_in_dim(points_all, wave_idx * band_rows, band_rows, 0)
    places = jnp.arange(ROWPAD, dtype=jnp.int32)
    inside = places[None, None, :] < out_points[None, :, None]
    return jnp.where(inside, result - climatology, 0.0)


def solution(mesh):
    placed = (
        P("wave", "lev", None),
        P("wave", None, None),
        P(),
        P(),
        P(),
        P(),
        P("lev", "wave", None),
    )
    return jax.shard_map(
        local, mesh=mesh, in_specs=placed, out_specs=P("lev", "wave", None), check_vma=False
    )
```

profile of v0, /device:TPU:0, one launch (start us, length us, event | category | flops | bytes accessed | tf_op | source)
XLA Modules:
  0.0 466.5 jit_solution(96725501821164234)
XLA Ops:
  0.0 0.8 dynamic_slice.27
  1.0 0.5 fusion.42
  1.5 14.9 %fusion.35 = f32[160,64,32]{1,2,0:T(8,128)S(1)} fusion(bf16[160,32,1280]{2,1,0:T(8,128)(2,1)} %param.10, bf16[160,64,1280]{2,1,0:T(8,128)(2,1)} %param.9, pred[160,1280]{1,0:T(8,128)(4,1)S(1)} %iota_compare_fusion.7), kind=kOutput, calls=%fused_computation.57 | convolution fusion | flops 851968000 | bytes 40837120 | tf_op jit(solution)/shard_map/scn,sjn->scj/dot_general | solution.py:84
  16.4 16.4 %fusion.33 = f32[160,64,32]{1,2,0:T(8,128)} fusion(bf16[160,32,1280]{2,1,0:T(8,128)(2,1)} %param.10, bf16[160,64,1280]{2,1,0:T(8,128)(2,1)} %param.9, pred[160,1280]{1,0:T(8,128)(4,1)S(1)} %iota_compare_fusion.7, bf16[160,1280]{1,0:T(8,128)(2,1)S(1)} %fusion.42), kind=kOutput, calls=%fused_computation.54 | convolution fusion | flops 865075200 | bytes 41246720 | tf_op jit(solution)/shard_map/scn,sjn->scj/dot_general | solution.py:87
  32.8 5.0 %pad_maximum_fusion = f32[160,64,64]{1,2,0:T(8,128)} fusion(f32[160,64,32]{1,2,0:T(8,128)} %fusion.33, f32[160,64,32]{1,2,0:T(8,128)S(1)} %fusion.35), kind=kLoop, calls=%fused_computation.61 | loop fusion | flops 655360 | bytes 5242880 | tf_op jit(solution)/shard_map/concatenate | solution.py:88
  37.8 6.3 %copy.19 = f32[160,64,64]{0,1,2:T(8,128)} copy(f32[160,64,64]{1,2,0:T(8,128)} %pad_maximum_fusion) | data formatting | bytes 5242880 | tf_op jit(solution)/shard_map/concatenate | solution.py:88
  44.1 100.5 %all_to_all.48 = f32[160,64,64]{0,1,2:T(8,128)S(1)} all-to-all(f32[160,64,64]{0,1,2:T(8,128)} %copy.19), channel_id=1, replica_groups=mesh['wave'=8,'lev'=4] {'wave'}, dimensions={2} | all-to-all | bytes 5242880 | tf_op jit(solution)/shard_map/all_to_all | solution.py:90
  144.5 4.4 copy.29
  148.9 4.0 all_to_all.38
  152.9 2.3 copy.21
  155.3 3.8 all-to-all-start.1
  159.3 31.1 %all-to-all-done.1 = f32[1280,64,8]{0,1,2:T(8,128)S(1)} async-done(((f32[1280,64,8]{0,1,2:T(8,128)}), f32[1280,64,8]{0,1,2:T(8,128)S(1)}, u32[]{:S(2)}, u32[]{:S(2)}) %all-to-all-start.1) | async-done | bytes 2621472 | tf_op jit(solution)/shard_map/all_to_all | solution.py:89
  190.3 1.7 copy.22
  192.1 264.9 %while.14 = (s32[]{:T(128)}, f32[2,4,5248]{2,0,1:T(2,128)}, s32[2]{0:T(128)S(1)}, s32[1280]{0:T(1024)S(1)}, f32[2,1280,256]{1,2,0:T(8,128)}, /*index=5*/s32[4]{0...) while((s32[]{:T(128)}, f32[2,4,5248]{2,0,1:T(2,128)}, ...), condition=%wide.region_3.4_spmd.clone, body=%wide.region_0.3_spmd.clone.sunk | while | flops 5220203520 | bytes 128362344 | solution.py:108
  192.1 0.7 dynamic_slice.34
  194.7 18.1 %fusion.77 = (f32[64,5248]{1,0:T(8,128)S(1)}, f32[64,5248]{1,0:T(8,128)S(1)}) fusion(f32[]{:T(128)S(6)} %div.27, s32[]{:T(128)S(6)} %select_n.194, pred[]{:T(512)S(6)} %lt.178), kind=kLoop, calls=%fused_computation.13.clone.1 | loop fusion | flops 3358720 | bytes 2686985 | tf_op jit(solution)/shard_map/while/body/eval_jaxpr/sin | solution.py:27
  212.8 6.9 %fusion.78 = (f32[20,5248]{1,0:T(8,128)S(1)}, f32[20,5248]{1,0:T(8,128)S(1)}) fusion(f32[]{:T(128)S(6)} %div.27, s32[]{:T(128)S(6)} %select_n.194, s32[20]{0:T(128)S(1)} %iota_multiply_fusion.2, pred[]{:T(512)S(6)} %lt.178), kind=kLoop, calls=%fused_computation.26.clone.1 | loop fusion | flops 1049600 | bytes 839769 | tf_op jit(solution)/shard_map/while/body/eval_jaxpr/cos | solution.py:28
  219.7 18.1 %multiply_add_fusion.2 = (f32[20,64,5248]{2,1,0:T(8,128)}, f32[20,64,5248]{2,1,0:T(8,128)}) fusion(f32[64,5248]{1,0:T(8,128)S(1)} %get-tuple-element.221, f32[20,5248]{1,0:T(8,128)S(1)} %get-tuple-element.222, f32[64,5248]{1,0:T(8,128)S(1)} %get-tuple-element.223, f32[20,5248]{1,0:T(8,128)S(1)} %get-tuple-element.224), kind=kLoop, calls=%fused_computation.2.clone.1 | loop fusion | flops 40304640 | bytes 57266176 | tf_op jit(solution)/shard_map/while/body/eval_jaxpr/add | solution.py:31
  238.4 1.4 constant_dynamic-slice_fusion.2
  239.9 1.5 convolution_bitcast_fusion.2
  241.7 1.3 copy.36
  243.0 0.4 broadcast.508
  243.4 33.1 %scatter_fusion = f32[1280,32,2]{1,2,0:T(2,128)S(1)} fusion(f32[1280,32,2]{1,2,0:T(2,128)S(1)} %broadcast.508, s32[1280]{0:T(1024)S(1)} %fusion.75, f32[1280,32,2]{1,2,0:T(2,128)S(1)} %copy.36), kind=kCustom, calls=%fused_computation.clone.clone.1 | custom fusion | bytes 988160 | tf_op jit(solution)/shard_map/while/body/eval_jaxpr/scatter | solution.py:35
  276.5 3.6 broadcast_multiply_fusion.2
  280.2 1.1 fusion.76
  281.2 19.6 %fusion.79 = f32[32,5248]{1,0:T(8,128)S(1)} fusion(f32[1280,32]{1,0:T(8,128)S(1)} %bitcast.65, f32[1280,5248]{1,0:T(8,128)} %bitcast.63), kind=kOutput, calls=%fused_computation.82.clone.1 | convolution fusion | flops 2579496960 | bytes 27705344 | tf_op jit(solution)/shard_map/while/body/eval_jaxpr/dot_general | solution.py:36
  300.8 0.6 iota_compare_fusion.10
  301.5 19.9 %fusion.80 = f32[32,5248]{1,0:T(8,128)S(1)} fusion(f32[32,5248]{1,0:T(8,128)S(1)} %fusion.79, f32[1280,32]{1,0:T(8,128)S(1)} %bitcast.66, f32[1280,5248]{1,0:T(8,128)} %bitcast.62, pred[5248]{0:T(1024)(128)(4,1)S(1)} %iota_compare_fusion.10), kind=kOutput, calls=%fused_computation.5.clone.1 | convolution fusion | flops 2579832832 | bytes 28382336 | tf_op jit(solution)/shard_map/while/body/eval_jaxpr/dot_general | solution.py:43
  321.9 1.9 dynamic_update_slice.10
  324.2 0.7 dynamic_slice.34
  326.8 17.8 %fusion.77 = (f32[64,5248]{1,0:T(8,128)S(1)}, f32[64,5248]{1,0:T(8,128)S(1)}) fusion(f32[]{:T(128)S(6)} %div.27, s32[]{:T(128)S(6)} %select_n.194, pred[]{:T(512)S(6)} %lt.178), kind=kLoop, calls=%fused_computation.13.clone.1 | loop fusion | flops 3358720 | bytes 2686985 | tf_op jit(solution)/shard_map/while/body/eval_jaxpr/sin | solution.py:27
  344.6 6.9 %fusion.78 = (f32[20,5248]{1,0:T(8,128)S(1)}, f32[20,5248]{1,0:T(8,128)S(1)}) fusion(f32[]{:T(128)S(6)} %div.27, s32[]{:T(128)S(6)} %select_n.194, s32[20]{0:T(128)S(1)} %iota_multiply_fusion.2, pred[]{:T(512)S(6)} %lt.178), kind=kLoop, calls=%fused_computation.26.clone.1 | loop fusion | flops 1049600 | bytes 839769 | tf_op jit(solution)/shard_map/while/body/eval_jaxpr/cos | solution.py:28
  351.5 18.1 %multiply_add_fusion.2 = (f32[20,64,5248]{2,1,0:T(8,128)}, f32[20,64,5248]{2,1,0:T(8,128)}) fusion(f32[64,5248]{1,0:T(8,128)S(1)} %get-tuple-element.221, f32[20,5248]{1,0:T(8,128)S(1)} %get-tuple-element.222, f32[64,5248]{1,0:T(8,128)S(1)} %get-tuple-element.223, f32[20,5248]{1,0:T(8,128)S(1)} %get-tuple-element.224), kind=kLoop, calls=%fused_computation.2.clone.1 | loop fusion | flops 40304640 | bytes 57266176 | tf_op jit(solution)/shard_map/while/body/eval_jaxpr/add | solution.py:31
  370.2 1.4 constant_dynamic-slice_fusion.2
  371.7 1.5 convolution_bitcast_fusion.2
  373.5 1.3 copy.36
  374.8 0.4 broadcast.508
  375.2 33.1 %scatter_fusion = f32[1280,32,2]{1,2,0:T(2,128)S(1)} fusion(f32[1280,32,2]{1,2,0:T(2,128)S(1)} %broadcast.508, s32[1280]{0:T(1024)S(1)} %fusion.75, f32[1280,32,2]{1,2,0:T(2,128)S(1)} %copy.36), kind=kCustom, calls=%fused_computation.clone.clone.1 | custom fusion | bytes 988160 | tf_op jit(solution)/shard_map/while/body/eval_jaxpr/scatter | solution.py:35
  408.3 3.6 broadcast_multiply_fusion.2
  412.0 1.1 fusion.76
  413.0 19.6 %fusion.79 = f32[32,5248]{1,0:T(8,128)S(1)} fusion(f32[1280,32]{1,0:T(8,128)S(1)} %bitcast.65, f32[1280,5248]{1,0:T(8,128)} %bitcast.63), kind=kOutput, calls=%fused_computation.82.clone.1 | convolution fusion | flops 2579496960 | bytes 27705344 | tf_op jit(solution)/shard_map/while/body/eval_jaxpr/dot_general | solution.py:36
  432.6 0.6 iota_compare_fusion.10
  433.3 20.0 %fusion.80 = f32[32,5248]{1,0:T(8,128)S(1)} fusion(f32[32,5248]{1,0:T(8,128)S(1)} %fusion.79, f32[1280,32]{1,0:T(8,128)S(1)} %bitcast.66, f32[1280,5248]{1,0:T(8,128)} %bitcast.62, pred[5248]{0:T(1024)(128)(4,1)S(1)} %iota_compare_fusion.10), kind=kOutput, calls=%fused_computation.5.clone.1 | convolution fusion | flops 2579832832 | bytes 28382336 | tf_op jit(solution)/shard_map/while/body/eval_jaxpr/dot_general | solution.py:43
  453.9 1.9 dynamic_update_slice.10
  457.0 3.4 all-to-all-start.2
  460.4 0.7 dynamic_slice.25
  461.1 4.3 all-to-all-done.2
  465.5 0.8 subtract_select_fusion
  (37 shorter events, 2.2 us)
Async XLA Ops:
  152.9 6.2 %copy-start.4 = (s32[32]{0:T(128)S(1)}, s32[32]{0:T(128)}, u32[]{:S(2)}) copy-start(s32[32]{0:T(128)} %param.12) | copy-start | bytes 388
  152.9 6.3 %copy-start.2 = (s32[4]{0:T(128)S(1)}, s32[4]{0:T(128)}, u32[]{:S(2)}) copy-start(s32[4]{0:T(128)} %param.13) | copy-start | bytes 52
  152.9 6.3 %copy-start.3 = (f32[4]{0:T(128)S(1)}, f32[4]{0:T(128)}, u32[]{:S(2)}) copy-start(f32[4]{0:T(128)} %param.14) | copy-start | bytes 52
  155.3 36.8 %copy-start = (s32[1280]{0:T(1024)S(1)}, s32[1280]{0:T(1024)}, u32[]{:S(2)}) copy-start(s32[1280]{0:T(1024)} %param.11) | copy-start | bytes 15364
  155.3 35.1 %all-to-all-start.1 = ((f32[1280,64,8]{0,1,2:T(8,128)}), f32[1280,64,8]{0,1,2:T(8,128)S(1)}, u32[]{:S(2)}, u32[]{:S(2)}) async-start(f32[1280,64,8]{0,1,2:T(8,128)} %copy.21), calls=%async_computation.1 | async-start | bytes 5242880 | tf_op jit(solution)/shard_map/all_to_all | solution.py:89
  159.2 32.9 %copy-start.5 = (s32[64]{0:T(128)}, s32[64]{0:T(128)S(1)}, u32[]{:S(2)}) copy-start(s32[64]{0:T(128)S(1)} %pad_add_fusion) | copy-start | bytes 772
  192.1 273.4 %copy-start.1 = (f32[1,8,5248]{2,1,0:T(8,128)S(1)}, f32[1,8,5248]{2,1,0:T(8,128)}, u32[]{:S(2)}) copy-start(f32[1,8,5248]{2,1,0:T(8,128)} %param.15) | copy-start | bytes 503812
  457.0 8.4 %all-to-all-start.2 = ((f32[4,2,5248]{2,1,0:T(2,128)}), f32[4,2,5248]{2,1,0:T(2,128)S(1)}, u32[]{:S(2)}, u32[]{:S(2)}) async-start(f32[4,2,5248]{2,1,0:T(2,128)} %bitcast.6), calls=%async_computation.2 | async-start | bytes 335872 | tf_op jit(solution)/shard_map/all_to_all | solution.py:110
where the time goes:
time: 475 us; the launch traced here: 467 us
  matrix products  113 us (24%)
  local copies, waits for them, and re-layouts  101 us (21%)
  other arithmetic  101 us (21%)
  blocking collectives  100 us (21%)
  waiting for transfers between devices  35.4 us (7%)
  starting transfers between devices  7.15 us (2%)
  loops' own time  7.07 us (1%)
    all_to_all x1, blocking collectives, local(): lax.all_to_all(fourier, 'wave', split_axis=2, concat_axis=0, tiled=True)  100 us
    scatter x2, local copies, waits for them, and re-layouts, synthesize(): jnp.zeros_like(coeffs).at[wave_map].set(coeffs) * factor[:, None, None]  66.2 us
    dot_general x2, matrix products, synthesize(): lax.dot_general(ordered[:, :, 1], sine_part, (((0,), (0,)), ((), ())), pr...  39.9 us
    dot_general x2, matrix products, synthesize(): lax.dot_general(ordered[:, :, 0], cosine, (((0,), (0,)), ((), ())), preci...  39.2 us
    add x2, other arithmetic, synthesize(): coarse_sin * fine_cos + coarse_cos * fine_sin  36.1 us
    sin x2, other arithmetic, synthesize(): fine_sin = jnp.sin(fine_angle)[None, :, :]  35.9 us
    all_to_all x1, waiting for transfers between devices, local(): lax.all_to_all(lax.all_to_all(fourier, 'wave', split_axis=2, concat_axis=...  31.1 us
    dot_general x1, matrix products, local(): jnp.einsum('scn,sjn->scj', signed, legendre, preferred_element_type=jnp.f...  16.4 us
  transfers between devices with their start and end apart: 2, of which 2 were waited for; matrix products, arithmetic and copies ran while one was open for 0% of the time, Pallas kernels for 0%

commit v1 on v0

v1 whole, which is shorter than its diff:
```python
import functools
import math

import jax
import jax.numpy as jnp
import numpy as np
from jax import lax
from jax.experimental import pallas as pl
from jax.experimental.pallas import tpu as pltpu
from jax.sharding import PartitionSpec as P

M = 1280
NT = 1280
LEV_DEV = 4
STEPS = 4
FIELDS = 2
ROWPAD = 5248

FS = FIELDS * STEPS
PART = 2 * FS
SQ = 8
HALF_M = M // 2
KPTS = 768
KBLK = 256
BUF = 1536
VMEM_LIMIT = 56 * 1024 * 1024
F32 = jnp.float32
BF16 = jnp.bfloat16


def iota(shape, dim):
    return lax.broadcasted_iota(jnp.int32, shape, dim)


def legendre_kernel(slots, wave_map, brackets, low_ref, up_ref, first_ref, leg_ref, weight_ref, own_ref, prev_ref):
    step = pl.program_id(0)
    groups = slots // SQ
    half = leg_ref.shape[2]
    wave = lax.axis_index("wave")
    lev = lax.axis_index("lev")
    degree = iota((16, NT), 1)
    sign = (1 - 2 * (degree % 2)).astype(F32).astype(BF16)
    row = iota((2 * half, 1), 0)
    lows, ups, firsts = [], [], []
    for sq in range(SQ):
        m = wave_map[wave * slots + sq * groups + step]
        kept = jnp.where(degree >= m, 1.0, 0.0).astype(BF16)
        leg = leg_ref[sq, 0]
        plain = jnp.concatenate([leg[i : i + 16] * kept for i in range(0, half, 16)], axis=0)
        signed = jnp.concatenate([plain[i : i + 16] * sign for i in range(0, half, 16)], axis=0)
        lhs = jnp.concatenate([plain, signed], axis=0)
        rhs = jnp.concatenate([low_ref[sq, 0], up_ref[sq, 0], first_ref[sq, 0]], axis=0)
        sums = lax.dot_general(lhs, rhs, (((1,), (1,)), ((), ())), preferred_element_type=F32)
        parity = (1 - 2 * (m % 2)).astype(F32)
        sums = sums * jnp.where(row < half, 1.0, parity)
        lows.append(sums[:, :PART])
        ups.append(sums[:, PART : 2 * PART])
        firsts.append(sums[:, 2 * PART :])
    lower = brackets[lev]
    has_upper = lower - lev * LEV_DEV < LEV_DEV - 1
    w = weight_ref[lev]
    upper_w = jnp.where(has_upper, 1.0 - w, 0.0)
    before = jnp.maximum(lev - 1, 0)
    crosses = (lev > 0) & (brackets[before] == lev * LEV_DEV - 1)
    first_w = jnp.where(crosses, 1.0 - weight_ref[before], 0.0)
    own_ref[0] = w * jnp.concatenate(lows, axis=1) + upper_w * jnp.concatenate(ups, axis=1)
    prev_ref[0] = first_w * jnp.concatenate(firsts, axis=1)


def legendre_sums(spectral, legendre, wave_map, brackets, lev_weight):
    slots, cols, _ = spectral.shape
    half = legendre.shape[1]
    groups = slots // SQ
    spec = spectral.reshape(SQ, groups, cols, NT)
    leg = legendre.reshape(SQ, groups, half, NT)

    def low_map(i, wm, br):
        lev = lax.axis_index("lev")
        return 0, i, br[lev] - lev * LEV_DEV, 0

    def up_map(i, wm, br):
        lev = lax.axis_index("lev")
        return 0, i, jnp.minimum(br[lev] - lev * LEV_DEV + 1, LEV_DEV - 1), 0

    spec_block = (SQ, 1, PART, NT)
    out = jax.ShapeDtypeStruct((groups, 2 * half, SQ * PART), F32)
    out_spec = pl.BlockSpec((1, 2 * half, SQ * PART), lambda i, wm, br: (i, 0, 0))
    return pl.pallas_call(
        functools.partial(legendre_kernel, slots),
        out_shape=[out, out],
        grid_spec=pltpu.PrefetchScalarGridSpec(
            num_scalar_prefetch=2,
            grid=(groups,),
            in_specs=[
                pl.BlockSpec(spec_block, low_map),
                pl.BlockSpec(spec_block, up_map),
                pl.BlockSpec(spec_block, lambda i, wm, br: (0, i, 0, 0)),
                pl.BlockSpec((SQ, 1, half, NT), lambda i, wm, br: (0, i, 0, 0)),
                pl.BlockSpec(memory_space=pltpu.SMEM),
            ],
            out_specs=[out_spec, out_spec],
        ),
        compiler_params=pltpu.CompilerParams(vmem_limit_bytes=VMEM_LIMIT),
        cost_estimate=pl.CostEstimate(flops=2 * slots * 2 * half * 48 * NT, bytes_accessed=slots * NT * 2 * (48 + half), transcendentals=0),
        name="legendre_sums",
    )(wave_map, brackets, spec, spec, spec, leg, lev_weight)


def unit_circle(product, quarter):
    turn = jnp.round(product * (1.0 / quarter))
    rest = product - turn * quarter
    x = rest * ((0.5 * math.pi) / quarter)
    x2 = x * x
    sine = x * (1.0 + x2 * (-1.0 / 6 + x2 * (1.0 / 120 + x2 * (-1.0 / 5040 + x2 * (1.0 / 362880)))))
    cosine = 1.0 + x2 * (-0.5 + x2 * (1.0 / 24 + x2 * (-1.0 / 720 + x2 * (1.0 / 40320))))
    quad = turn.astype(jnp.int32) & 3
    odd = (quad & 1) == 1
    c = jnp.where(odd, sine, cosine)
    s = jnp.where(odd, cosine, sine)
    c = jnp.where((quad == 1) | (quad == 2), -c, c)
    s = jnp.where(quad >= 2, -s, s)
    return c, s


def own_points(points_ref, r2):
    wave = lax.axis_index("wave")
    lev = lax.axis_index("lev")
    band = 2 * lax.axis_size("lev")
    row = wave * band + r2 * lax.axis_size("lev") + lev
    return points_ref[row % points_ref.shape[0]]


def table_kernel(points_ref, map_ref, hi_ref, lo_ref, perm_ref):
    r2 = pl.program_id(0)
    kb = pl.program_id(1)
    rows = hi_ref.shape[1]
    steps = pl.num_programs(1)
    quarter = (own_points(points_ref, r2) // 4).astype(F32)
    perm_rows = perm_ref.shape[0]
    order = (r2 * steps + kb) * perm_rows + iota((perm_rows, M), 0)
    wanted = jnp.where(order < HALF_M, 2 * order, 2 * (order - HALF_M) + 1)
    perm_ref[...] = jnp.where(map_ref[...] == wanted, 1.0, 0.0).astype(BF16)

    def put(tile, chunk, value):
        lanes = slice(tile * 128, tile * 128 + 128)
        hi = value.astype(BF16)
        hi_ref[0, pl.ds(chunk, 16), lanes] = hi
        lo_ref[0, pl.ds(chunk, 16), lanes] = (value - hi.astype(F32)).astype(BF16)

    def chunk_body(i, carry):
        chunk = pl.multiple_of(i * 16, 16)
        k = (kb * rows + chunk + iota((16, 128), 0)).astype(F32)
        lane = iota((16, 128), 1).astype(F32)
        c, s = unit_circle(2.0 * lane * k, quarter)
        c1, s1 = unit_circle(k, quarter)
        ct, st = unit_circle(256.0 * k, quarter)
        co = c * c1 - s * s1
        so = s * c1 + c * s1
        for t in range(HALF_M // 128):
            if t:
                c, s = c * ct - s * st, s * ct + c * st
                co, so = co * ct - so * st, so * ct + co * st
            put(t, chunk, c)
            put(5 + t, chunk, s)
            put(10 + t, chunk, co)
            put(15 + t, chunk, so)
        return carry

    lax.fori_loop(0, rows // 16, chunk_body, 0)


def tables(row_points, slot_map):
    steps = 8
    rows = KPTS // steps
    table = jax.ShapeDtypeStruct((2, KPTS, 2 * M), BF16)
    table_spec = pl.BlockSpec((1, rows, 2 * M), lambda r, k: (r, k, 0))
    return pl.pallas_call(
        table_kernel,
        out_shape=[table, table, jax.ShapeDtypeStruct((M, M), BF16)],
        grid=(2, steps),
        in_specs=[pl.BlockSpec(memory_space=pltpu.SMEM), pl.BlockSpec(memory_space=pltpu.VMEM)],
        out_specs=[table_spec, table_spec, pl.BlockSpec((M // (2 * steps), M), lambda r, k: (r * steps + k, 0))],
        compiler_params=pltpu.CompilerParams(vmem_limit_bytes=VMEM_LIMIT),
        cost_estimate=pl.CostEstimate(flops=2 * KPTS * 2 * M * 12, bytes_accessed=2 * KPTS * 2 * M * 4 + M * M * 2, transcendentals=0),
        name="fourier_tables",
    )(row_points, slot_map)


def pick_tables(plev):
    wide = plev * 2 * PART
    out = np.zeros((2, 4, 2 * wide, 2 * wide), np.float32)
    plans = (
        ((0, 1), (0, 1), (0, 1), (0, 1)),
        ((1, -1), (1, 1), (1, -1), (1, 1)),
        ((0, 1), (0, 1), (1, -1), (1, -1)),
        ((1, -1), (1, 1), (0, -1), (0, 1)),
    )
    for r2 in range(2):
        for kind, plan in enumerate(plans):
            for image, (part, sgn) in enumerate(plan):
                for hl in range(2):
                    for p in range(plev):
                        for q in range(FS):
                            src = hl * wide + p * 2 * PART + r2 * PART + q * 2 + part
                            dst = hl * wide + image * plev * FS + p * FS + q
                            out[r2, kind, src, dst] = sgn
    return out.astype(jnp.bfloat16)


def mean_table(plev):
    wide = plev * FS * 4
    out = np.zeros((2 * 4 * plev, 2 * wide), np.float32)
    for quarter in range(4):
        for p in range(plev):
            for part in range(2):
                image_quarter = (quarter + part) % 4
                start = (image_quarter * 2 + part) * plev * FS + p * FS
                out[part * 4 * plev + quarter * plev + p, start : start + FS] = 0.5 / STEPS
    return out.astype(jnp.bfloat16)


def flip_table():
    return np.fliplr(np.eye(KBLK, dtype=np.float32)).astype(jnp.bfloat16)


def split(x):
    hi = x.astype(BF16)
    return hi, (x - hi.astype(F32)).astype(BF16)


def nt_dot(a, b):
    return lax.dot_general(a, b, (((1,), (1,)), ((), ())), preferred_element_type=F32)


def nn_dot(a, b):
    return jnp.dot(a, b, preferred_element_type=F32)


def synth_kernel(points_ref, moved_ref, perm_ref, hi_ref, lo_ref, pick_ref, mean_ref, flip_ref, out_ref, mixed, coef, direct, mirror, line):
    r2 = pl.program_id(0)
    kb = pl.program_id(1)
    waves, plev, block_rows, _ = moved_ref.shape
    sub = block_rows // 2
    wide = plev * 2 * PART
    part_rows = waves * sub

    @pl.when((r2 == 0) & (kb == 0))
    def _():
        for base in range(0, plev * 2, 8):
            cur = []
            for g in range(base, base + 8):
                pieces = [moved_ref[w, g // 2, (g % 2) * sub : (g % 2 + 1) * sub, :] for w in range(waves)]
                cur.append(jnp.concatenate(pieces, axis=0))
            group = iota((part_rows, 128), 1) // PART
            for bit in (1, 2, 4):
                unset = (group & bit) == 0
                nxt = list(cur)
                for g in range(8):
                    if g & bit == 0:
                        a, b = cur[g], cur[g + bit]
                        nxt[g] = jnp.where(unset, a, pltpu.roll(b, bit * PART, 1))
                        nxt[g + bit] = jnp.where(unset, pltpu.roll(a, 128 - bit * PART, 1), b)
                cur = nxt
            for sq in range(SQ):
                hi, lo = split(cur[sq])
                lane = base * PART
                mixed[sq * part_rows : (sq + 1) * part_rows, lane : lane + 128] = hi
                mixed[sq * part_rows : (sq + 1) * part_rows, wide + lane : wide + lane + 128] = lo

        lane_row = (iota((1, 2 * wide), 1) // PART) % 2
        limit0 = (own_points(points_ref, 0) - 1) // 2
        limit1 = (own_points(points_ref, 1) - 1) // 2
        limit = jnp.where(lane_row == 0, limit0, limit1)
        place = iota((HALF_M, 1), 0)
        turned = (iota((1, 2 * wide), 1) % wide) // (plev * FS) >= 2
        flip_sign = jnp.where(turned & (place % 2 == 1), -1.0, 1.0).astype(BF16)
        for odd in range(2):
            ordered = nn_dot(perm_ref[odd * HALF_M : (odd + 1) * HALF_M, :], mixed[...])
            wave = 2 * place + odd
            factor = jnp.where(wave <= limit, jnp.where(wave == 0, 1.0, 2.0), 0.0)
            ordered = (ordered * factor).astype(BF16)
            for row in range(2):
                for part in range(2):
                    picked = nn_dot(ordered, pick_ref[row, odd * 2 + part]).astype(BF16)
                    coef[row, odd, part * HALF_M : (part + 1) * HALF_M, :] = picked * flip_sign
        direct[...] = jnp.zeros_like(direct)
        mirror[...] = jnp.zeros_like(mirror)

    def contraction(odd):
        lanes = slice(odd * M, (odd + 1) * M)
        both = nn_dot(hi_ref[0, :, lanes], coef[r2, odd])
        rest = nn_dot(lo_ref[0, :, lanes], coef[r2, odd, :, :wide])
        return both[:, :wide] + (both[:, wide:] + rest)

    even_sum = contraction(0)
    odd_sum = contraction(1)
    plus = even_sum + odd_sum
    minus = even_sum - odd_sum
    squares = jnp.concatenate([plus * plus, minus * minus], axis=1)
    sq_hi, sq_lo = split(squares)
    energy = nt_dot(mean_ref[...], sq_hi) + nt_dot(mean_ref[...], sq_lo)
    rows = 4 * plev
    direct[:, pl.ds(pl.multiple_of(kb * KBLK, KBLK), KBLK)] = energy[:rows]
    en_hi, en_lo = split(energy[rows:])
    back = KPTS // KBLK - 1 - kb
    mirror[:, pl.ds(pl.multiple_of(back * KBLK, KBLK), KBLK)] = nn_dot(en_hi, flip_ref[...]) + nn_dot(en_lo, flip_ref[...])

    @pl.when(kb == KPTS // KBLK - 1)
    def _():
        quarter = own_points(points_ref, r2) // 4
        lane = iota((rows, BUF), 1)
        shift = (quarter + (BUF - (KPTS - 1))) % BUF
        whole = jnp.where(lane <= quarter // 2, direct[...], pltpu.roll(mirror[...], shift, 1))
        direct[...] = whole
        line[...] = jnp.zeros_like(line)
        lane = iota((plev, BUF), 1)
        for b in range(4):
            start = quarter * b
            inner = start % 128
            base = pl.multiple_of(start - inner, 128)
            piece = pltpu.roll(direct[b * plev : (b + 1) * plev, :], inner, 1)
            old = line[:, pl.ds(base, BUF)]
            line[:, pl.ds(base, BUF)] = jnp.where((lane >= inner) & (lane < inner + quarter), piece, old)
        out_ref[:, pl.ds(r2, 1), :] = line[:, :ROWPAD].reshape(plev, 1, ROWPAD)


def synthesis(moved, perm, table_hi, table_lo, row_points):
    waves, plev, block_rows, _ = moved.shape
    wide = plev * 2 * PART
    steps = KPTS // KBLK
    table_spec = pl.BlockSpec((1, KBLK, 2 * M), lambda r, k: (r, k, 0))
    vmem = pl.BlockSpec(memory_space=pltpu.VMEM)
    return pl.pallas_call(
        synth_kernel,
        out_shape=jax.ShapeDtypeStruct((plev, 2, ROWPAD), F32),
        grid=(2, steps),
        in_specs=[pl.BlockSpec(memory_space=pltpu.SMEM), vmem, vmem, table_spec, table_spec, vmem, vmem, vmem],
        out_specs=vmem,
        scratch_shapes=[
            pltpu.VMEM((M, 2 * wide), BF16),
            pltpu.VMEM((2, 2, M, 2 * wide), BF16),
            pltpu.VMEM((4 * plev, BUF), F32),
            pltpu.VMEM((4 * plev, BUF), F32),
            pltpu.VMEM((plev, 3 * 1280 + BUF), F32),
        ],
        compiler_params=pltpu.CompilerParams(vmem_limit_bytes=VMEM_LIMIT),
        cost_estimate=pl.CostEstimate(flops=2 * 2 * KPTS * 2 * M * 384, bytes_accessed=2 * KPTS * 2 * M * 4 + M * M * 2, transcendentals=0),
        name="synthesis",
    )(row_points, moved, perm, table_hi, table_lo, pick_tables(plev), mean_table(plev), flip_table())


def local(spectral, legendre, wave_map, row_points, brackets, lev_weight, climatology):
    slots = spectral.shape[0]
    half = legendre.shape[1]
    groups = slots // SQ
    wave_count = lax.axis_size("wave")
    lev_count = lax.axis_size("lev")
    rows_dev = 2 * half // (wave_count * lev_count)
    own, prev = legendre_sums(spectral, legendre, wave_map, brackets, lev_weight)
    from_next = lax.ppermute(prev, "lev", [(d, d - 1) for d in range(1, lev_count)])
    sums = (own + from_next).reshape(groups, wave_count, rows_dev, lev_count, SQ * PART)
    sums = jnp.transpose(sums, (1, 3, 2, 0, 4)).reshape(wave_count * lev_count, rows_dev * groups, SQ * PART)
    moved = lax.all_to_all(sums, ("wave", "lev"), split_axis=0, concat_axis=0, tiled=True)
    moved = moved.reshape(wave_count, lev_count, rows_dev * groups, SQ * PART)
    slot_map = jnp.transpose(wave_map.reshape(wave_count, SQ, groups), (1, 0, 2)).reshape(1, M)
    table_hi, table_lo, perm = tables(row_points, slot_map)
    energy = synthesis(moved, perm, table_hi, table_lo, row_points)
    result = lax.all_to_all(energy, "lev", split_axis=0, concat_axis=0, tiled=True)
    result = jnp.transpose(result, (1, 0, 2)).reshape(1, rows_dev * lev_count, ROWPAD)
    points_all = jnp.concatenate([row_points, row_points])
    band_rows = rows_dev * lev_count
    out_points = lax.dynamic_slice_in_dim(points_all, lax.axis_index("wave") * band_rows, band_rows, 0)
    places = jnp.arange(ROWPAD, dtype=jnp.int32)
    inside = places[None, None, :] < out_points[None, :, None]
    return jnp.where(inside, result - climatology, 0.0)


def solution(mesh):
    placed = (
        P("wave", "lev", None),
        P("wave", None, None),
        P(),
        P(),
        P(),
        P(),
        P("lev", "wave", None),
    )
    return jax.shard_map(
        local, mesh=mesh, in_specs=placed, out_specs=P("lev", "wave", None), check_vma=False
    )
```

time: 475 us -> 89.6 us (0.19); the launches traced: 467 us -> 88.6 us
  matrix products: 113 us -> 0 us
  blocking collectives: 100 us -> 0 us
  other arithmetic: 101 us -> 2 us
  local copies, waits for them, and re-layouts: 101 us -> 3.25 us
  Pallas kernels: 0 us -> 55.7 us
  waiting for transfers between devices: 35.4 us -> 9.16 us
  starting transfers between devices: 7.15 us -> 18.4 us
  loops' own time: 7.07 us -> 0 us
    dot_general x8 -> x0, matrix products: 113 us -> none  [the longest x2 39.9 us: synthesize(): lax.dot_general(ordered[:, :, 1], sine_part, (((0,), (0,)), ((), ())), pr...]
    all_to_all x1 -> x0, blocking collectives: 100 us -> none  [local(): lax.all_to_all(fourier, 'wave', split_axis=2, concat_axis=0, tiled=True)]
    scatter x2 -> x0, local copies, waits for them, and re-layouts: 66.2 us -> none  [synthesize(): jnp.zeros_like(coeffs).at[wave_map].set(coeffs) * factor[:, None, None]]
    pallas_call x0 -> x3, Pallas kernels: none -> 55.7 us  [the longest x1 23.6 us: legendre_sums(): pl.pallas_call(functools.partial(legendre_kernel, slots), out_shape=[out,...]
    sin x2 -> x0, other arithmetic: 35.9 us -> none  [synthesize(): fine_sin = jnp.sin(fine_angle)[None, :, :]]
    add x3 -> x1, other arithmetic: 36.1 us -> 1.17 us  [local(): own + from_next]
    all_to_all x2, waiting for transfers between devices: 35.4 us -> 6.26 us  [the longest x1 4.82 us: local(): lax.all_to_all(energy, 'lev', split_axis=0, concat_axis=0, tiled=True)]
    cos x2 -> x0, other arithmetic: 13.8 us -> none  [synthesize(): coarse_cos = jnp.cos(coarse_angle)[:, None, :]]
  transfers between devices with their start and end apart: 2 -> 3, of which waited for: 2 -> 3; matrix products, arithmetic and copies ran while one was open for 0% -> 1% of each run, Pallas kernels for 0% -> 18%
where the time goes in v1:
time: 89.6 us; the launch traced here: 88.6 us
  Pallas kernels  55.7 us (62%)
  starting transfers between devices  18.4 us (21%)
  waiting for transfers between devices  9.16 us (10%)
  local copies, waits for them, and re-layouts  3.25 us (4%)
  other arithmetic  2 us (2%)
    pallas_call x1, Pallas kernels, legendre_sums(): pl.pallas_call(functools.partial(legendre_kernel, slots), out_shape=[out,...  23.6 us
    pallas_call x1, Pallas kernels, synthesis(): pl.pallas_call(synth_kernel, out_shape=jax.ShapeDtypeStruct((plev, 2, ROW...  16.5 us
    pallas_call x1, Pallas kernels, tables(): pl.pallas_call(table_kernel, out_shape=[table, table, jax.ShapeDtypeStruc...  15.6 us
    all_to_all x1, starting transfers between devices, local(): lax.all_to_all(sums, ('wave', 'lev'), split_axis=0, concat_axis=0, tiled=...  13.8 us
    all_to_all x1, waiting for transfers between devices, local(): lax.all_to_all(energy, 'lev', split_axis=0, concat_axis=0, tiled=True)  4.82 us
    all_to_all x1, starting transfers between devices, local(): lax.all_to_all(energy, 'lev', split_axis=0, concat_axis=0, tiled=True)  3.35 us
    ppermute x1, waiting for transfers between devices, local(): lax.ppermute(prev, 'lev', [(d, d - 1) for d in range(1, lev_count)])  2.9 us
  transfers between devices with their start and end apart: 3, of which 3 were waited for; matrix products, arithmetic and copies ran while one was open for 1% of the time, Pallas kernels for 18%

profile of v1, /device:TPU:0, one launch (start us, length us, event | category | flops | bytes accessed | tf_op | source)
XLA Modules:
  0.0 88.6 jit_solution(9045373960451727235)
XLA Ops:
  0.0 0.0 copy-start.2
  0.0 23.6 %legendre_sums.1 = (f32[20,64,128]{2,1,0:T(8,128)}, f32[20,64,128]{2,1,0:T(8,128)}) custom-call(s32[1280]{0:T(1024)} %wave_map.1, s32[4]{0:T(128)} %brackets.1, bf16[8,20,64,1280]{3,2,1,0:T(8,128)(2,1)} %bitcast.9, bf16[8,20,64,1280]{3,2,1,0:T(8,128)(2,1)} %bitcast.10, bf16[8,20,64,1280]{3,2,1,0:T(8,128)(2,1)} %bitcast.11, ...), custom_call_target="tpu_custom_call" | custom-call | flops 1258291200 | bytes 32768000 | tf_op jit(solution)/shard_map/legendre_sums/pallas_call | solution.py:88
  23.6 1.3 %collective-permute-start = (f32[20,64,128]{2,1,0:T(8,128)}, f32[20,64,128]{2,1,0:T(8,128)S(1)}, u32[]{:S(2)}, u32[]{:S(2)}) collective-permute-start(f32[20,64,128]{2,1,0:T(8,128)} %get-tuple-element.11), channel_id=1, source_target_pairs={{1,0},{2,1},{3,2},{5,4},{6,5},{7,6},{9,8},{10,9},{11,10},{13,12},{... | collective-permute-start | bytes 1966088 | tf_op jit(solution)/shard_map/ppermute | solution.py:360
  24.9 2.9 %collective-permute-done = f32[20,64,128]{2,1,0:T(8,128)S(1)} collective-permute-done((f32[20,64,128]{2,1,0:T(8,128)}, f32[20,64,128]{2,1,0:T(8,128)S(1)}, u32[]{:S(2)}, u32[]{:S(2)}) %collective-permute-start) | collective-permute-done | bytes 655392 | tf_op jit(solution)/shard_map/ppermute | solution.py:360
  27.8 1.2 %add.7 = f32[20,64,128]{2,1,0:T(8,128)S(1)} add(f32[20,64,128]{2,1,0:T(8,128)} %get-tuple-element.10, f32[20,64,128]{2,1,0:T(8,128)S(1)} %collective-permute-done) | non-fusion elementwise | flops 163840 | bytes 1966080 | tf_op jit(solution)/shard_map/add | solution.py:361
  28.9 0.2 copy.16
  29.1 1.2 %copy.17 = f32[32,40,128]{2,1,0:T(8,128)} copy(f32[32,40,128]{2,0,1:T(8,128)S(1)} %bitcast.14) | data formatting | bytes 1310720 | tf_op jit(solution)/shard_map/reshape | solution.py:362
  30.4 13.8 %all-to-all-start = ((f32[32,40,128]{2,1,0:T(8,128)}), f32[32,40,128]{2,1,0:T(8,128)S(1)}, u32[]{:S(2)}, u32[]{:S(2)}) async-start(f32[32,40,128]{2,1,0:T(8,128)} %copy.17), calls=%async_computation | async-start | bytes 1310720 | tf_op jit(solution)/shard_map/all_to_all | solution.py:363
  44.1 0.0 copy-done.2
  44.1 0.1 reshape.61
  44.3 0.7 reshape.62.map_ref
  45.0 15.6 %fourier_tables.1 = (bf16[2,768,2560]{2,1,0:T(8,128)(2,1)}, bf16[2,768,2560]{2,1,0:T(8,128)(2,1)}, bf16[1280,1280]{1,0:T(8,128)(2,1)}) custom-call(s32[32]{0:T(128)} %points_ref.3, s32[1,1280]{1,0:T(1,128)} %reshape.62.map_ref), custom_call_target="tpu_custom_call" | custom-call | flops 47185920 | bytes 19005440 | tf_op jit(solution)/shard_map/fourier_tables/pallas_call | solution.py:177
  60.6 1.4 %all-to-all-done = f32[32,40,128]{2,1,0:T(8,128)S(1)} async-done(((f32[32,40,128]{2,1,0:T(8,128)}), f32[32,40,128]{2,1,0:T(8,128)S(1)}, u32[]{:S(2)}, u32[]{:S(2)}) %all-to-all-start) | async-done | bytes 655392 | tf_op jit(solution)/shard_map/all_to_all | solution.py:363
  62.0 0.0 copy-start
  62.0 0.8 copy-done
  62.9 0.0 copy-start.3
  62.9 0.0 copy-start.1
  62.9 16.5 %synthesis.1 = f32[4,2,5248]{2,1,0:T(2,128)} custom-call(s32[32]{0:T(128)} %points_ref.3, f32[8,4,40,128]{3,2,1,0:T(8,128)} %bitcast.13, bf16[1280,1280]{1,0:T(8,128)(2,1)} %get-tuple-element.12.perm_ref, bf16[2,768,2560]{2,1,0:T(8,128)(2,1)} %get-tuple-element.13.hi_ref, bf16[2,768,2560]{2,1,0:T(8,128)(2,1)} %get-tuple-element.14.lo_ref, ...), custom_call_target="tpu_custom_call" | custom-call | flops 3019898880 | bytes 19005440 | tf_op jit(solution)/shard_map/synthesis/pallas_call | solution.py:333
  79.4 3.3 %all-to-all-start.1 = ((f32[4,2,5248]{2,1,0:T(2,128)}), f32[4,2,5248]{2,1,0:T(2,128)S(1)}, u32[]{:S(2)}, u32[]{:S(2)}) async-start(f32[4,2,5248]{2,1,0:T(2,128)} %synthesis.1), calls=%async_computation.1 | async-start | bytes 335872 | tf_op jit(solution)/shard_map/all_to_all | solution.py:368
  82.8 0.0 copy-done.3
  82.8 0.1 pad_add_fusion
  82.8 0.1 dynamic_slice.3
  82.9 4.8 %all-to-all-done.1 = f32[4,2,5248]{2,1,0:T(2,128)S(1)} async-done(((f32[4,2,5248]{2,1,0:T(2,128)}), f32[4,2,5248]{2,1,0:T(2,128)S(1)}, u32[]{:S(2)}, u32[]{:S(2)}) %all-to-all-start.1) | async-done | bytes 167968 | tf_op jit(solution)/shard_map/all_to_all | solution.py:368
  87.8 0.1 reshape.63
  87.9 0.0 copy-done.1
  87.9 0.8 subtract_select_fusion
  (2 shorter events, 0.1 us)
Async XLA Ops:
  0.0 44.1 %copy-start.2 = (s32[1280]{0:T(1024)S(1)}, s32[1280]{0:T(1024)}, u32[]{:S(2)}) copy-start(s32[1280]{0:T(1024)} %wave_map.1) | copy-start | bytes 15364
  23.6 4.2 %collective-permute-start = (f32[20,64,128]{2,1,0:T(8,128)}, f32[20,64,128]{2,1,0:T(8,128)S(1)}, u32[]{:S(2)}, u32[]{:S(2)}) collective-permute-start(f32[20,64,128]{2,1,0:T(8,128)} %get-tuple-element.11), channel_id=1, source_target_pairs={{1,0},{2,1},{3,2},{5,4},{6,5},{7,6},{9,8},{10,9},{11,10},{13,12},{... | collective-permute-start | bytes 1966088 | tf_op jit(solution)/shard_map/ppermute | solution.py:360
  30.4 31.7 %all-to-all-start = ((f32[32,40,128]{2,1,0:T(8,128)}), f32[32,40,128]{2,1,0:T(8,128)S(1)}, u32[]{:S(2)}, u32[]{:S(2)}) async-start(f32[32,40,128]{2,1,0:T(8,128)} %copy.17), calls=%async_computation | async-start | bytes 1310720 | tf_op jit(solution)/shard_map/all_to_all | solution.py:363
  62.0 0.8 copy-start
  62.9 19.9 %copy-start.3 = (s32[32]{0:T(128)S(1)}, s32[32]{0:T(128)}, u32[]{:S(2)}) copy-start(s32[32]{0:T(128)} %points_ref.3) | copy-start | bytes 388
  62.9 25.0 %copy-start.1 = (f32[1,8,5248]{2,1,0:T(8,128)S(1)}, f32[1,8,5248]{2,1,0:T(8,128)}, u32[]{:S(2)}) copy-start(f32[1,8,5248]{2,1,0:T(8,128)} %param.16) | copy-start | bytes 503812
  79.4 8.3 %all-to-all-start.1 = ((f32[4,2,5248]{2,1,0:T(2,128)}), f32[4,2,5248]{2,1,0:T(2,128)S(1)}, u32[]{:S(2)}, u32[]{:S(2)}) async-start(f32[4,2,5248]{2,1,0:T(2,128)} %synthesis.1), calls=%async_computation.1 | async-start | bytes 335872 | tf_op jit(solution)/shard_map/all_to_all | solution.py:368
